TPU v7x, 32 devices: a whole 2x2x4 slice. The times are simulated.
32 devices in a mesh: grp: 2 (over core), aux: 4 (over y, x), orb: 4 (over z).
Axes of the slice: x: 2, y: 2, z: 4, core: 2. Of those that a mesh axis runs over, the one named last changes fastest.
Arguments:
- fitted_tensor: bfloat16 [4, 8192, 8192], P('grp', 'aux', 'orb'), may hold values from -0.23925781 to 0.23925781
- block_mask: int32 [2, 64, 64], P('grp'), may hold values 0 or 1
- orbitals: bfloat16 [8192, 256], P('aux'), may hold values from -0.0625 to 0.0625
- nuclear: float32 [8192], replicated, may hold values from 0.5 to 1.5
- centres: float32 [3, 8192], replicated, may hold values from 0 to 8
- mm_positions: float32 [3, 32768], P(None, ('grp', 'aux', 'orb')), may hold values from 0 to 8
- mm_charges: float32 [32768], P(('grp', 'aux', 'orb')), may hold values from -0.12 to 0.12
- neighbours: int32 [32, 2], P(('grp', 'aux', 'orb')), may hold values from 0 to 63, all different within a row
Outputs:
- fock: float32 [8192, 8192], P(('aux', 'orb'))
- mm_potential: float32 [32768], P(('grp', 'aux', 'orb'))
Inputs may be any that keep to these rules, and one draw needn't show every extreme that they name: `neighbours`: each row names 2 different blocks; every block is named by some row.
All inputs are finite; a program needn't handle non-finite values. No bound on the sum of `block_mask` on one device may be relied on, other than what follows from the above.
Results may differ from a plain program's by a relative error of at most 0.01.
Values may be sent and summed in bfloat16 or wider, within the bound.
A program may use at most 128 MiB of HBM per device.

v0:
```python
import jax
import jax.numpy as jnp
from jax import lax
from jax.sharding import PartitionSpec as P

BLK = 128
softening = 1.0


def near_kernel(picker, centre_blocks, charge_blocks, atom_xyz):
    near_xyz = jnp.einsum("kb,cbj->ckj", picker, centre_blocks, precision=lax.Precision.HIGHEST)
    near_xyz = near_xyz.reshape(3, picker.shape[0] * centre_blocks.shape[2])
    near_q = jnp.dot(picker, charge_blocks, precision=lax.Precision.HIGHEST).reshape(-1)
    offsets = near_xyz[:, :, None] - atom_xyz[:, None, :]
    kernel = lax.rsqrt(jnp.sum(offsets * offsets, axis=0) + softening)
    return (kernel, near_q)


def add_diagonal(fock_rows, first_row, field_vec):
    row_count = fock_rows.shape[0]
    values = lax.dynamic_slice_in_dim(field_vec, first_row, row_count, 0)
    row_ids = jnp.arange(row_count, dtype=jnp.int32)[:, None]
    col_ids = jnp.arange(fock_rows.shape[1], dtype=jnp.int32)[None, :]
    on_diagonal = col_ids == first_row + row_ids
    return fock_rows + jnp.where(on_diagonal, values[:, None], jnp.float32(0.0))


def block_picker(first, count, block_total):
    positions = (first + jnp.arange(count, dtype=jnp.int32)) // BLK
    block_ids = jnp.arange(block_total, dtype=jnp.int32)
    return (positions[:, None] == block_ids[None, :]).astype(jnp.float32)


def per_device(
    fitted_tensor, block_mask, orbitals, nuclear, centres, mm_positions, mm_charges, neighbours
):
    row_span = fitted_tensor.shape[1]
    col_span = fitted_tensor.shape[2]
    orb_count = lax.axis_size("orb")
    aux_id = lax.axis_index("aux")
    orb_id = lax.axis_index("orb")
    own_span = row_span // orb_count
    block_total = block_mask.shape[1]
    whole_c = lax.all_gather(orbitals, "aux", axis=0, tiled=True)
    row_start = aux_id * row_span
    col_start = orb_id * col_span
    window_c = lax.dynamic_slice_in_dim(whole_c, col_start, col_span, 0)
    row_pick = block_picker(row_start, row_span, block_total)
    col_pick = block_picker(col_start, col_span, block_total)
    row_bits = jnp.dot(row_pick, block_mask[0].astype(jnp.float32), precision=lax.Precision.HIGHEST)
    mask_wide = jnp.dot(row_bits, col_pick.T, precision=lax.Precision.HIGHEST).astype(jnp.bfloat16)
    masked = fitted_tensor * mask_wide[None]
    x_partial = jnp.einsum("pmn,ni->pmi", masked, window_c, preferred_element_type=jnp.float32)
    x_rows = lax.psum(x_partial, "orb")
    own_rows = lax.dynamic_slice_in_dim(x_rows, orb_id * own_span, own_span, 1)
    x_own = own_rows.astype(jnp.bfloat16)
    own_c = lax.dynamic_slice_in_dim(orbitals, orb_id * own_span, own_span, 0)
    dens_part = 2.0 * jnp.einsum("pmi,mi->p", x_own, own_c, preferred_element_type=jnp.float32)
    densities = lax.psum(dens_part, ("aux", "orb")).astype(jnp.bfloat16)
    coulomb_block = jnp.einsum("pmn,p->mn", masked, densities, preferred_element_type=jnp.float32)
    coulomb = lax.all_to_all(coulomb_block, "orb", split_axis=0, concat_axis=1, tiled=True)
    c_float = whole_c.astype(jnp.float32)
    population = 2.0 * jnp.sum(c_float * c_float, axis=1)
    qm_charge = nuclear - population
    centre_blocks = centres.reshape(3, block_total, BLK)
    charge_blocks = qm_charge.reshape(block_total, BLK)
    picker = (neighbours[0][:, None] == jnp.arange(block_total, dtype=jnp.int32)[None, :]).astype(
        jnp.float32
    )
    kernel, near_q = near_kernel(picker, centre_blocks, charge_blocks, mm_positions)
    mm_potential = jnp.dot(near_q, kernel, precision=lax.Precision.HIGHEST)
    contrib = jnp.dot(kernel, mm_charges, precision=lax.Precision.HIGHEST).reshape(
        picker.shape[0], BLK
    )
    field_part = jnp.dot(picker.T, contrib, precision=lax.Precision.HIGHEST)
    field_sum = lax.psum(field_part, ("grp", "aux", "orb"))
    field_vec = field_sum.reshape(-1)
    own_first = row_start + orb_id * own_span
    exchange_part = jnp.einsum(
        "pmi,pni->mn",
        x_own,
        lax.all_gather(x_own, ("aux", "orb"), axis=1, tiled=True),
        preferred_element_type=jnp.float32,
    )
    fock_part = coulomb - 0.5 * exchange_part
    fock_sum = lax.psum(fock_part, "grp")
    fock = add_diagonal(fock_sum, own_first, field_vec)
    return (fock, mm_potential)


def solution(mesh):
    in_specs = (
        P("grp", "aux", "orb"),
        P("grp", None, None),
        P("aux", None),
        P(),
        P(),
        P(None, ("grp", "aux", "orb")),
        P(("grp", "aux", "orb")),
        P(("grp", "aux", "orb"), None),
    )
    out_specs = (P(("aux", "orb"), None), P(("grp", "aux", "orb")))
    return jax.shard_map(
        per_device, mesh=mesh, in_specs=in_specs, out_specs=out_specs, check_vma=False
    )
```

profile of v0, /device:TPU:0, one launch (start us, length us, event | category | flops | bytes accessed | tf_op | source)
XLA Modules:
  0.0 848.3 jit_solution(9946186388667584154)
XLA Ops:
  7.2 0.0 copy-start
  7.2 0.0 all-gather.3.cloned.1.call-start
  7.2 0.7 all-gather.3.cloned.1.call-update
  8.0 1.0 bitcast_convert_fusion
  9.0 1.7 fusion.6
  10.6 7.5 convolution_convert_fusion
  18.1 14.8 %broadcast_multiply_fusion = bf16[2,2048,2048]{2,1,0:T(8,128)(2,1)} fusion(bf16[2,2048,2048]{2,1,0:T(8,128)(2,1)} %param.8, bf16[2048,2048]{1,0:T(8,128)(2,1)S(1)} %convolution_convert_fusion), kind=kLoop, calls=%fused_computation.7 | loop fusion | flops 8388608 | bytes 41943040 | tf_op jit(solution)/shard_map/mul | solution.py:52
  32.9 32.4 %all-gather.3.cloned.1.call-done = bf16[8192,256]{1,0:T(8,128)(2,1)} async-done(((bf16[2048,256]{1,0:T(8,128)(2,1)}), bf16[8192,256]{1,0:T(8,128)(2,1)}) %all-gather.3.cloned.1.call-update) | async-done | bytes 4194320 | tf_op jit(solution)/shard_map/all_gather | solution.py:44
  65.3 12.5 %fusion.3 = f32[2,2048,256]{2,1,0:T(8,128)} fusion(bf16[2,2048,2048]{2,1,0:T(8,128)(2,1)} %broadcast_multiply_fusion, bf16[8192,256]{1,0:T(8,128)(2,1)} %all-gather.3.cloned.1.call-done, s32[]{:T(128)S(6)} %select_n.32), kind=kOutput, calls=%fused_computation.12 | convolution fusion | flops 4294967296 | bytes 22020100 | tf_op jit(solution)/shard_map/pmn,ni->pmi/dot_general | solution.py:53
  77.8 147.1 %all-reduce.4 = bf16[2,2048,256]{2,1,0:T(8,128)(2,1)S(1)} all-reduce(f32[2,2048,256]{2,1,0:T(8,128)} %fusion.3), channel_id=1, replica_groups=mesh['grp'=2,'aux'=4,'orb'=4] {'orb'}, use_global_device_ids=true, to_apply=%region_0.1 | all-reduce | flops 1048576 | bytes 6291456 | tf_op jit(solution)/shard_map/psum | solution.py:54
  224.9 1.0 multiply_reduce_fusion.2
  225.9 38.2 %psum.29 = bf16[2]{0:T(256)(128)(2,1)S(1)} all-reduce(f32[2]{0:T(128)S(1)} %broadcast_multiply_fusion.1), channel_id=1, replica_groups=mesh['grp'=2,'aux'=4,'orb'=4] {'aux','orb'}, use_global_device_ids=true, to_apply=%region_1.2 | all-reduce | flops 2 | bytes 12 | tf_op jit(solution)/shard_map/psum | solution.py:59
  264.2 28.8 %fusion.1 = f32[1,2048,2048]{2,0,1:T(1,128)S(1)} fusion(bf16[2,2048,2048]{2,1,0:T(8,128)(2,1)} %broadcast_multiply_fusion, bf16[2]{0:T(256)(128)(2,1)S(1)} %psum.29), kind=kOutput, calls=%fused_computation.4 | convolution fusion | flops 16777216 | bytes 33554436 | tf_op jit(solution)/shard_map/pmn,p->mn/dot_general | solution.py:60
  292.9 11.3 %copy.18 = f32[1,2048,2048]{2,1,0:T(8,128)} copy(f32[1,2048,2048]{2,0,1:T(1,128)S(1)} %fusion.1) | data formatting | bytes 33554432 | tf_op jit(solution)/shard_map/pmn,p->mn/dot_general | solution.py:60
  304.2 7.0 all-to-all-start
  311.2 0.0 all-gather.5.cloned.1.call-start
  311.2 0.7 all-gather.5.cloned.1.call-update
  312.0 0.0 all-reduce.3.cloned.1.call-start
  312.0 433.2 %all-to-all-done = f32[4,512,2048]{2,1,0:T(8,128)} async-done(((f32[4,512,2048]{2,1,0:T(8,128)}), f32[4,512,2048]{2,1,0:T(8,128)}, u32[]{:S(2)}, u32[]{:S(2)}) %all-to-all-start) | async-done | bytes 16777248 | tf_op jit(solution)/shard_map/all_to_all | solution.py:61
  745.2 0.0 copy-start.1
  745.2 11.9 %copy.21 = f32[4,64,8,2048]{3,2,0,1:T(8,128)} copy(f32[4,64,8,2048]{3,2,1,0:T(8,128)} %bitcast.23) | data formatting | bytes 33554432 | tf_op jit(solution)/shard_map/all_to_all | solution.py:61
  757.0 0.0 all-gather.5.cloned.1.call-done
  757.0 0.0 copy-done.1
  757.0 14.4 %fusion = f32[512,8192]{1,0:T(8,128)} fusion(f32[512,8192]{1,0:T(8,128)} %bitcast.59, bf16[2,512,256]{2,1,0:T(8,128)(2,1)S(1)} %copy-done.1, bf16[2,8192,256]{2,1,0:T(8,128)(2,1)} %all-gather.5.cloned.1.call-done), kind=kOutput, calls=%fused_computation.1 | convolution fusion | flops 4303355904 | bytes 42467328 | tf_op jit(solution)/shard_map/pmi,pni->mn/dot_general | solution.py:79
  771.4 0.0 copy-start.2
  771.4 0.0 copy-start.5
  771.4 0.0 copy-start.4
  771.4 0.0 copy-start.3
  771.5 0.0 all-reduce.3.cloned.1.call-update
  771.5 0.9 copy-done.2
  772.3 0.0 copy-done.5
  772.3 0.2 convolution_bitcast_fusion.1
  772.5 0.0 copy-done.4
  772.5 0.4 multiply_reduce_fusion.1
  772.9 0.0 copy-done
  772.9 1.0 fusion.8
  773.9 0.3 convolution_bitcast_fusion
  774.2 37.3 %psum.31 = f32[8192]{0:T(1024)S(1)} all-reduce(f32[8192]{0:T(1024)S(1)} %convolution_bitcast_fusion), channel_id=1, replica_groups=mesh['grp'=2,'aux'=4,'orb'=4] {'grp','aux','orb'}, use_global_device_ids=true, to_apply=%region_4.5 | all-reduce | flops 8192 | bytes 65536 | tf_op jit(solution)/shard_map/psum | solution.py:76
  811.5 0.1 dynamic_slice.15
  811.6 3.8 multiply_reduce_fusion
  815.3 0.0 copy-done.3
  815.3 0.2 fusion.15
  815.5 1.3 fusion.7
  816.8 12.9 %all-reduce.3.cloned.1.call-done = f32[512,8192]{1,0:T(8,128)} async-done(((f32[512,8192]{1,0:T(8,128)}), f32[512,8192]{1,0:T(8,128)}) %all-reduce.3.cloned.1.call-update) | async-done | bytes 16777232 | tf_op jit(solution)/shard_map/psum | solution.py:86
  829.7 12.1 %select_add_fusion = f32[512,8192]{1,0:T(8,128)} fusion(f32[512,8192]{1,0:T(8,128)} %all-reduce.3.cloned.1.call-done, f32[512]{0:T(512)S(1)} %dynamic_slice.15, s32[512]{0:T(512)S(1)} %iota_add_fusion.2), kind=kLoop, calls=%fused_computation.2 | loop fusion | flops 12582912 | bytes 33558528 | tf_op jit(solution)/shard_map/add | solution.py:25
  (5 shorter events, 0.0 us)
Async XLA Ops:
  7.2 765.8 %copy-start = (f32[1024]{0:T(1024)S(1)}, f32[1024]{0:T(1024)}, u32[]{:S(2)}) copy-start(f32[1024]{0:T(1024)} %param.14) | copy-start | bytes 12292
  7.2 58.1 %all-gather.3.cloned.1.call-start = ((), (), s32[]{:S(2)}) async-start(), calls=%async_computation.1 | async-start | bytes 5242880 | tf_op jit(solution)/shard_map/all_gather | solution.py:44
  304.2 440.9 %all-to-all-start = ((f32[4,512,2048]{2,1,0:T(8,128)}), f32[4,512,2048]{2,1,0:T(8,128)}, u32[]{:S(2)}, u32[]{:S(2)}) async-start(f32[4,512,2048]{2,1,0:T(8,128)} %bitcast.58), calls=%async_computation | async-start | bytes 33554432 | tf_op jit(solution)/shard_map/all_to_all | solution.py:61
  311.2 445.8 %all-gather.5.cloned.1.call-start = ((), (), s32[]{:S(2)}) async-start(), calls=%async_computation.2 | async-start | bytes 8912896 | tf_op jit(solution)/shard_map/all_gather | solution.py:82
  312.0 517.8 %all-reduce.3.cloned.1.call-start = ((), (), s32[]{:S(2)}) async-start(), calls=%async_computation.3 | async-start | bytes 33554432 | tf_op jit(solution)/shard_map/psum | solution.py:86
  745.2 11.9 %copy-start.1 = (bf16[2,512,256]{2,1,0:T(8,128)(2,1)S(1)}, bf16[2,512,256]{2,1,0:T(8,128)(2,1)}, u32[]{:S(2)}) copy-start(bf16[2,512,256]{2,1,0:T(8,128)(2,1)} %get-tuple-element.3) | copy-start | bytes 1572868
  771.4 0.9 copy-start.2
  771.4 0.9 copy-start.5
  771.4 1.1 copy-start.4
  771.4 43.9 %copy-start.3 = (f32[8192]{0:T(1024)S(1)}, f32[8192]{0:T(1024)}, u32[]{:S(2)}) copy-start(f32[8192]{0:T(1024)} %param.11) | copy-start | bytes 98308
Sparse Core Ops, SparseCore 0:
  9.9 55.3 all-gather.2
  314.8 381.6 all-gather.4
  771.6 58.0 all-reduce.2
where the time goes:
time: 849 us; the launch traced here: 848 us
  waiting for transfers between devices  480 us (57%)
  blocking collectives  223 us (26%)
  matrix products  67.7 us (8%)
  other arithmetic  33.1 us (4%)
  local copies, waits for them, and re-layouts  24.2 us (3%)
  between operations  13.9 us (2%)
    all_to_all x1, waiting for transfers between devices, per_device(): lax.all_to_all(coulomb_block, 'orb', split_axis=0, concat_axis=1, tiled=T...  433 us
    psum x1, blocking collectives, per_device(): x_rows = lax.psum(x_partial, 'orb')  147 us
    psum x1, blocking collectives, per_device(): densities = lax.psum(dens_part, ('aux', 'orb')).astype(jnp.bfloat16)  38.2 us
    psum x1, blocking collectives, per_device(): field_sum = lax.psum(field_part, ('grp', 'aux', 'orb'))  37.3 us
    all_gather x1, waiting for transfers between devices, per_device(): whole_c = lax.all_gather(orbitals, 'aux', axis=0, tiled=True)  32.4 us
    dot_general x1, matrix products, per_device(): jnp.einsum('pmn,p->mn', masked, densities, preferred_element_type=jnp.flo...  28.8 us
  transfers between devices with their start and end apart: 4, of which 3 were waited for; matrix products, arithmetic and copies ran while one was open for 5% of the time, Pallas kernels for 0%

commit v1 on v0

--- a/solution.py
+++ b/solution.py
@@ -51,7 +51,9 @@
     mask_wide = jnp.dot(row_bits, col_pick.T, precision=lax.Precision.HIGHEST).astype(jnp.bfloat16)
     masked = fitted_tensor * mask_wide[None]
     x_partial = jnp.einsum("pmn,ni->pmi", masked, window_c, preferred_element_type=jnp.float32)
-    x_rows = lax.psum(x_partial, "orb")
+    x_rows = x_partial
+    for hop in (1, 2):
+        x_rows = x_rows + lax.ppermute(x_rows, "orb", [(dev, dev ^ hop) for dev in range(4)])
     own_rows = lax.dynamic_slice_in_dim(x_rows, orb_id * own_span, own_span, 1)
     x_own = own_rows.astype(jnp.bfloat16)
     own_c = lax.dynamic_slice_in_dim(orbitals, orb_id * own_span, own_span, 0)

time: 849 us -> 981 us (1.16)
  waiting for transfers between devices: 480 us -> 753 us
  blocking collectives: 223 us -> 78.4 us
    ppermute x0 -> x2, waiting for transfers between devices: none -> 270 us  [per_device(): lax.ppermute(x_rows, 'orb', [(dev, dev ^ hop) for dev in range(4)])]
    psum x1 -> x0, blocking collectives: 147 us -> none  [per_device(): x_rows = lax.psum(x_partial, 'orb')]
  transfers between devices with their start and end apart: 4 -> 6, of which waited for: 3 -> 5; matrix products, arithmetic and copies ran while one was open for 5% -> 4% of each run, Pallas kernels for 0% -> 0%
where the time goes in v1:
time: 981 us
  waiting for transfers between devices  753 us (77%)
  blocking collectives  78.4 us (8%)
  matrix products  63.8 us (7%)
  other arithmetic  36.9 us (4%)
  local copies, waits for them, and re-layouts  24.2 us (2%)
  between operations  13.9 us (1%)
  starting transfers between devices  11.1 us (1%)
    all_to_all x1, waiting for transfers between devices, per_device(): lax.all_to_all(coulomb_block, 'orb', split_axis=0, concat_axis=1, tiled=T...  435 us
    ppermute x2, waiting for transfers between devices, per_device(): lax.ppermute(x_rows, 'orb', [(dev, dev ^ hop) for dev in range(4)])  270 us
    psum x1, blocking collectives, per_device(): densities = lax.psum(dens_part, ('aux', 'orb')).astype(jnp.bfloat16)  41.1 us
    psum x1, blocking collectives, per_device(): field_sum = lax.psum(field_part, ('grp', 'aux', 'orb'))  37.3 us
    all_gather x1, waiting for transfers between devices, per_device(): whole_c = lax.all_gather(orbitals, 'aux', axis=0, tiled=True)  33.5 us
    dot_general x1, matrix products, per_device(): jnp.einsum('pmn,p->mn', masked, densities, preferred_element_type=jnp.flo...  28.8 us
  transfers between devices with their start and end apart: 6, of which 5 were waited for; matrix products, arithmetic and copies ran while one was open for 4% of the time, Pallas kernels for 0%

profile of v1, /device:TPU:0, one launch (start us, length us, event | category | flops | bytes accessed | tf_op | source)
XLA Modules:
  0.0 980.7 jit_solution(4316853738600085029)
XLA Ops:
  7.2 0.0 copy-start
  7.2 0.0 all-gather.3.cloned.1.call-start
  7.2 0.7 all-gather.3.cloned.1.call-update
  8.0 1.7 fusion.7
  9.6 7.5 convolution_convert_fusion
  17.1 14.7 %broadcast_multiply_fusion = bf16[2,2048,2048]{2,1,0:T(8,128)(2,1)} fusion(bf16[2,2048,2048]{2,1,0:T(8,128)(2,1)} %param.8, bf16[2048,2048]{1,0:T(8,128)(2,1)S(1)} %convolution_convert_fusion), kind=kLoop, calls=%fused_computation.7 | loop fusion | flops 8388608 | bytes 41943040 | tf_op jit(solution)/shard_map/mul | solution.py:52
  31.8 33.5 %all-gather.3.cloned.1.call-done = bf16[8192,256]{1,0:T(8,128)(2,1)} async-done(((bf16[2048,256]{1,0:T(8,128)(2,1)}), bf16[8192,256]{1,0:T(8,128)(2,1)}) %all-gather.3.cloned.1.call-update) | async-done | bytes 4194320 | tf_op jit(solution)/shard_map/all_gather | solution.py:44
  65.3 8.6 fusion.4
  73.9 1.6 collective-permute-start
  75.5 90.8 %collective-permute-done = f32[2,2048,256]{2,1,0:T(8,128)S(1)} collective-permute-done((f32[2,2048,256]{2,1,0:T(8,128)S(1)}, f32[2,2048,256]{2,1,0:T(8,128)S(1)}, u32[]{:S(2)}, u32[]{:S(2)}) %collective-permute-start) | collective-permute-done | bytes 4194336 | tf_op jit(solution)/shard_map/ppermute | solution.py:56
  166.3 2.5 add.80
  168.8 2.4 collective-permute-start.1
  171.2 1.0 bitcast_convert_fusion
  172.2 179.1 %collective-permute-done.1 = f32[2,2048,256]{2,1,0:T(8,128)} collective-permute-done((f32[2,2048,256]{2,1,0:T(8,128)}, f32[2,2048,256]{2,1,0:T(8,128)}, u32[]{:S(2)}, u32[]{:S(2)}) %collective-permute-start.1) | collective-permute-done | bytes 4194336 | tf_op jit(solution)/shard_map/ppermute | solution.py:56
  351.3 2.6 multiply_reduce_fusion.2
  353.9 41.1 %psum.21 = bf16[2]{0:T(256)(128)(2,1)S(1)} all-reduce(f32[2]{0:T(128)S(1)} %broadcast_multiply_fusion.1), channel_id=1, replica_groups=mesh['grp'=2,'aux'=4,'orb'=4] {'aux','orb'}, use_global_device_ids=true, to_apply=%region_0.1 | all-reduce | flops 2 | bytes 12 | tf_op jit(solution)/shard_map/psum | solution.py:61
  395.0 28.8 %fusion.1 = f32[1,2048,2048]{2,0,1:T(1,128)S(1)} fusion(bf16[2,2048,2048]{2,1,0:T(8,128)(2,1)} %broadcast_multiply_fusion, bf16[2]{0:T(256)(128)(2,1)S(1)} %psum.21), kind=kOutput, calls=%fused_computation.4 | convolution fusion | flops 16777216 | bytes 33554436 | tf_op jit(solution)/shard_map/pmn,p->mn/dot_general | solution.py:62
  423.8 11.3 %copy.18 = f32[1,2048,2048]{2,1,0:T(8,128)} copy(f32[1,2048,2048]{2,0,1:T(1,128)S(1)} %fusion.1) | data formatting | bytes 33554432 | tf_op jit(solution)/shard_map/pmn,p->mn/dot_general | solution.py:62
  435.1 7.0 all-to-all-start
  442.1 0.0 all-gather.5.cloned.1.call-start
  442.1 0.7 all-gather.5.cloned.1.call-update
  442.8 0.0 all-reduce.2.cloned.1.call-start
  442.9 434.7 %all-to-all-done = f32[4,512,2048]{2,1,0:T(8,128)} async-done(((f32[4,512,2048]{2,1,0:T(8,128)}), f32[4,512,2048]{2,1,0:T(8,128)}, u32[]{:S(2)}, u32[]{:S(2)}) %all-to-all-start) | async-done | bytes 16777248 | tf_op jit(solution)/shard_map/all_to_all | solution.py:63
  877.5 0.0 copy-start.1
  877.5 11.9 %copy.21 = f32[4,64,8,2048]{3,2,0,1:T(8,128)} copy(f32[4,64,8,2048]{3,2,1,0:T(8,128)} %bitcast.23) | data formatting | bytes 33554432 | tf_op jit(solution)/shard_map/all_to_all | solution.py:63
  889.4 0.0 all-gather.5.cloned.1.call-done
  889.4 0.0 copy-done.1
  889.4 14.4 %fusion = f32[512,8192]{1,0:T(8,128)} fusion(f32[512,8192]{1,0:T(8,128)} %bitcast.59, bf16[2,512,256]{2,1,0:T(8,128)(2,1)S(1)} %copy-done.1, bf16[2,8192,256]{2,1,0:T(8,128)(2,1)} %all-gather.5.cloned.1.call-done), kind=kOutput, calls=%fused_computation.1 | convolution fusion | flops 4303355904 | bytes 42467328 | tf_op jit(solution)/shard_map/pmi,pni->mn/dot_general | solution.py:81
  903.8 0.0 copy-start.2
  903.8 0.0 copy-start.5
  903.8 0.0 copy-start.3
  903.8 0.0 all-reduce.2.cloned.1.call-update
  903.8 0.9 copy-done.2
  904.7 0.0 copy-done.5
  904.7 0.2 convolution_bitcast_fusion.1
  904.9 0.0 copy-done.4
  904.9 0.4 multiply_reduce_fusion.1
  905.3 0.0 copy-done
  905.3 1.0 fusion.9
  906.2 0.3 convolution_bitcast_fusion
  906.6 37.3 %psum.23 = f32[8192]{0:T(1024)S(1)} all-reduce(f32[8192]{0:T(1024)S(1)} %convolution_bitcast_fusion), channel_id=1, replica_groups=mesh['grp'=2,'aux'=4,'orb'=4] {'grp','aux','orb'}, use_global_device_ids=true, to_apply=%region_3.4 | all-reduce | flops 8192 | bytes 65536 | tf_op jit(solution)/shard_map/psum | solution.py:78
  943.8 0.1 dynamic_slice.15
  943.9 3.8 multiply_reduce_fusion
  947.7 0.0 copy-done.3
  947.7 0.2 fusion.16
  947.9 1.3 fusion.8
  949.1 13.0 %all-reduce.2.cloned.1.call-done = f32[512,8192]{1,0:T(8,128)} async-done(((f32[512,8192]{1,0:T(8,128)}), f32[512,8192]{1,0:T(8,128)}) %all-reduce.2.cloned.1.call-update) | async-done | bytes 16777232 | tf_op jit(solution)/shard_map/psum | solution.py:88
  962.1 12.1 %select_add_fusion = f32[512,8192]{1,0:T(8,128)} fusion(f32[512,8192]{1,0:T(8,128)} %all-reduce.2.cloned.1.call-done, f32[512]{0:T(512)S(1)} %dynamic_slice.15, s32[512]{0:T(512)S(1)} %iota_add_fusion.2), kind=kLoop, calls=%fused_computation.2 | loop fusion | flops 12582912 | bytes 33558528 | tf_op jit(solution)/shard_map/add | solution.py:25
  (6 shorter events, 0.0 us)
Async XLA Ops:
  7.2 898.1 %copy-start = (f32[1024]{0:T(1024)S(1)}, f32[1024]{0:T(1024)}, u32[]{:S(2)}) copy-start(f32[1024]{0:T(1024)} %param.14) | copy-start | bytes 12292
  7.2 58.1 %all-gather.3.cloned.1.call-start = ((), (), s32[]{:S(2)}) async-start(), calls=%async_computation.1 | async-start | bytes 5242880 | tf_op jit(solution)/shard_map/all_gather | solution.py:44
  73.9 92.4 %collective-permute-start = (f32[2,2048,256]{2,1,0:T(8,128)S(1)}, f32[2,2048,256]{2,1,0:T(8,128)S(1)}, u32[]{:S(2)}, u32[]{:S(2)}) collective-permute-start(f32[2,2048,256]{2,1,0:T(8,128)S(1)} %fusion.4), channel_id=1, source_target_pairs={{0,1},{1,0},{2,3},{3,2},{4,5},{5,4},{6,7},{7,6},{8,9},{9,8},{10,11... | collective-permute-start | bytes 12582920 | tf_op jit(solution)/shard_map/ppermute | solution.py:56
  168.8 182.5 %collective-permute-start.1 = (f32[2,2048,256]{2,1,0:T(8,128)}, f32[2,2048,256]{2,1,0:T(8,128)}, u32[]{:S(2)}, u32[]{:S(2)}) collective-permute-start(f32[2,2048,256]{2,1,0:T(8,128)} %add.80), channel_id=1, source_target_pairs={{0,2},{1,3},{2,0},{3,1},{4,6},{5,7},{6,4},{7,5},{8,10},{9,11},{10,... | collective-permute-start | bytes 12582920 | tf_op jit(solution)/shard_map/ppermute | solution.py:56
  435.1 442.4 %all-to-all-start = ((f32[4,512,2048]{2,1,0:T(8,128)}), f32[4,512,2048]{2,1,0:T(8,128)}, u32[]{:S(2)}, u32[]{:S(2)}) async-start(f32[4,512,2048]{2,1,0:T(8,128)} %bitcast.58), calls=%async_computation | async-start | bytes 33554432 | tf_op jit(solution)/shard_map/all_to_all | solution.py:63
  442.1 447.3 %all-gather.5.cloned.1.call-start = ((), (), s32[]{:S(2)}) async-start(), calls=%async_computation.2 | async-start | bytes 8912896 | tf_op jit(solution)/shard_map/all_gather | solution.py:84
  442.8 519.3 %all-reduce.2.cloned.1.call-start = ((), (), s32[]{:S(2)}) async-start(), calls=%async_computation.3 | async-start | bytes 33554432 | tf_op jit(solution)/shard_map/psum | solution.py:88
  877.5 11.9 %copy-start.1 = (bf16[2,512,256]{2,1,0:T(8,128)(2,1)S(1)}, bf16[2,512,256]{2,1,0:T(8,128)(2,1)}, u32[]{:S(2)}) copy-start(bf16[2,512,256]{2,1,0:T(8,128)(2,1)} %get-tuple-element.3) | copy-start | bytes 1572868
  903.8 0.9 copy-start.2
  903.8 0.9 copy-start.5
  903.8 1.1 copy-start.4
  903.8 43.9 %copy-start.3 = (f32[8192]{0:T(1024)S(1)}, f32[8192]{0:T(1024)}, u32[]{:S(2)}) copy-start(f32[8192]{0:T(1024)} %param.11) | copy-start | bytes 98308
Sparse Core Ops, SparseCore 0:
  9.9 55.3 all-gather.2
  445.7 383.3 all-gather.4
  904.0 58.1 all-reduce.1
